TPU v7x, 32 devices: a whole 2x2x4 slice. The times are simulated.
32 devices in a mesh: section: 2 (over core), seq: 4 (over z), head: 4 (over y, x).
Axes of the slice: x: 2, y: 2, z: 4, core: 2. Of those that a mesh axis runs over, the one named last changes fastest.
Arguments:
- query_vectors: bfloat16 [2, 512, 8192], P('section', 'seq', 'head'), may hold values from -400 to 400
- key_vectors: bfloat16 [2, 512, 8192], P('section', 'seq', 'head'), may hold values from -6 to 6
- value_vectors: bfloat16 [2, 512, 8192], P('section', 'seq', 'head'), may hold values from -6 to 6
- prior_state: float32 [2, 64, 128, 128], P('section', 'head'), may hold values from -64 to 64
- doc_ids: int32 [2, 512], P('section', 'seq'), may hold values from 0 to 3, never falling along the last dimension, each value on 1 to 256 neighbouring positions
- norm_gain: float32 [2, 8192], P('section', 'head'), may hold values from 0.25 to 1.75
- residual: bfloat16 [2, 512, 6144], P('section', 'head', 'seq'), may hold values from -6 to 6
- out_weight: bfloat16 [2, 8192, 6144], P('section', 'head', 'seq'), may hold values from -0.0625 to 0.0625
- enc_weight: bfloat16 [2, 6144, 32768], P('section', None, ('seq', 'head')), may hold values from -0.078125 to 0.078125
- enc_bias: float32 [2, 32768], P('section', ('seq', 'head')), may hold values from -5 to 5
Outputs:
- handoff: bfloat16 [2, 512, 6144], P('section', 'head', 'seq')
- monitor: bfloat16 [2, 8, 32768], P('section', None, ('seq', 'head'))
Inputs may be any that keep to these rules, and one draw needn't show every extreme that they name: `doc_ids`: document numbers never fall along a section's tokens, are 0 at its first token and rise by at most 1 from one token to the next; a document has at most 256 tokens, and one has exactly that many.
All inputs are finite; a program needn't handle non-finite values.
Results may differ from a plain program's by a relative error of at most 0.0039.
Values may be sent and summed in bfloat16 or wider, within the bound.
A program may use at most 128 MiB of HBM per device.

v0:
```python
import jax
import jax.numpy as jnp
from jax import lax
from jax.sharding import PartitionSpec as P

HD = 128
POOL = 64
HDIM = 8192


epsilon = 1e-06


def entering(part, axis, combine, identity):
    place = lax.axis_index(axis)
    gathered = jax.tree.map(lambda a: lax.all_gather(a, axis), part)
    state = jax.tree.map(lambda a, e: jnp.zeros_like(a) + jnp.asarray(e, a.dtype), part, identity)

    def one(hop, state):
        return combine(
            state, jax.tree.map(lambda a: lax.dynamic_index_in_dim(a, hop, 0, False), gathered)
        )

    return lax.fori_loop(0, place, one, state)


def passed_along(x, axis, by):
    devices = lax.axis_size(axis)
    return lax.ppermute(x, axis, [(i, (i + by) % devices) for i in range(devices)])


def merge_states(first_pair, second_pair):
    first_state, first_doc = first_pair
    second_state, second_doc = second_pair
    top_doc = jnp.maximum(first_doc, second_doc)
    merged = jnp.where(first_doc == top_doc, first_state, 0.0) + jnp.where(
        second_doc == top_doc, second_state, 0.0
    )
    return (merged, top_doc)


def local(
    query_vectors,
    key_vectors,
    value_vectors,
    prior_state,
    doc_ids,
    norm_gain,
    residual,
    out_weight,
    enc_weight,
    enc_bias,
):
    highest = lax.Precision.HIGHEST
    row_count = query_vectors.shape[1]
    local_heads = query_vectors.shape[2] // HD
    queries = query_vectors[0].reshape(row_count, local_heads, HD)
    keys_block = key_vectors[0].reshape(row_count, local_heads, HD)
    values_block = value_vectors[0].reshape(row_count, local_heads, HD)
    doc_index = doc_ids[0]
    doc_float = doc_index.astype(jnp.float32)
    last_doc = doc_float[-1]
    keys_last = jnp.where(
        (doc_index == doc_index[-1])[:, None, None], keys_block, jnp.zeros_like(keys_block)
    )
    summary = jnp.einsum(
        "thd,the->hde", keys_last, values_block, preferred_element_type=jnp.float32
    )
    identity_pair = (jnp.zeros_like(summary), jnp.full((1,), -1.0, jnp.float32))
    earlier_state, earlier_last = entering(
        (summary, last_doc[None]), "seq", merge_states, identity_pair
    )
    earlier_doc = earlier_last[0]
    incoming_state, incoming_doc = merge_states(
        (prior_state[0], jnp.zeros((), jnp.float32)), (earlier_state, earlier_doc)
    )
    inter = jnp.einsum(
        "thd,hde->the", queries.astype(jnp.float32), incoming_state, precision=highest
    )
    inter = inter * (doc_float == incoming_doc).astype(jnp.float32)[:, None, None]
    scores = jnp.einsum("thd,uhd->htu", queries, keys_block, preferred_element_type=jnp.float32)
    positions = jnp.arange(row_count)
    same_doc = (positions[None, :] <= positions[:, None]) & (
        doc_index[:, None] == doc_index[None, :]
    )
    scores = jnp.where(same_doc[None, :, :], scores, 0.0)
    intra = jnp.einsum("htu,uhe->the", scores, values_block.astype(jnp.float32), precision=highest)
    attended = (inter + intra).reshape(row_count, local_heads * HD)
    total_square = lax.psum(jnp.sum(attended * attended, axis=1), "head")
    inverse_rms = lax.rsqrt(total_square / HDIM + epsilon)
    normed = (attended * inverse_rms[:, None] * norm_gain[0]).astype(jnp.bfloat16)
    projection = out_weight[0]
    partial_sums = jnp.dot(
        lax.all_gather(normed, "seq", axis=0, tiled=True),
        projection,
        preferred_element_type=jnp.float32,
    )
    own_rows = residual[0]
    encoder = enc_weight[0]
    latent_width = encoder.shape[1]
    reduced = lax.psum_scatter(partial_sums, "head", scatter_dimension=0, tiled=True)
    layer_out = (own_rows.astype(jnp.float32) + reduced).astype(jnp.bfloat16)
    features = lax.all_gather(layer_out, "head", axis=0, tiled=True)
    pre_scores = jnp.dot(
        lax.all_gather(features, "seq", axis=1, tiled=True),
        encoder,
        preferred_element_type=jnp.float32,
    )
    latent = jax.nn.relu(pre_scores + enc_bias[0])
    pooled = jnp.mean(latent.reshape(-1, POOL, latent_width), axis=1).astype(jnp.bfloat16)
    handoff, monitor = passed_along((layer_out[None], pooled[None]), "section", 1)
    return (handoff, monitor)


def solution(mesh):
    return jax.shard_map(
        local,
        mesh=mesh,
        in_specs=(
            P("section", "seq", "head"),
            P("section", "seq", "head"),
            P("section", "seq", "head"),
            P("section", "head", None, None),
            P("section", "seq"),
            P("section", "head"),
            P("section", "head", "seq"),
            P("section", "head", "seq"),
            P("section", None, ("seq", "head")),
            P("section", ("seq", "head")),
        ),
        out_specs=(P("section", "head", "seq"), P("section", None, ("seq", "head"))),
        check_vma=False,
    )
```

profile of v0, /device:TPU:0, one launch (start us, length us, event | category | flops | bytes accessed | tf_op | source)
XLA Modules:
  0.0 395.7 jit_solution(4831983781017161528)
XLA Ops:
  7.2 0.0 copy-start.5
  7.2 0.0 copy-start.3
  7.2 0.0 copy-start
  7.2 0.0 all-gather.13.cloned.1.call-start
  7.2 1.3 slice.8
  8.5 1.3 broadcast_compare_fusion
  9.8 1.3 copy.23
  11.2 1.3 copy.24
  12.5 1.4 fusion.14
  13.9 0.0 all-gather.13.cloned.1.call-update
  13.9 0.0 all-gather.7.cloned.1.call-start
  14.0 0.0 copy-done.5
  14.0 0.6 dynamic-slice
  14.6 0.0 copy-done.3
  14.6 0.8 slice_dynamic-update-slice_fusion
  15.4 13.5 %all-reduce = f32[4]{0:T(128)S(1)} all-reduce(f32[4]{0:T(128)S(1)} %slice_dynamic-update-slice_fusion), channel_id=2, replica_groups=mesh['section'=2,'seq'=4,'head'=4] {'seq'}, use_global_device_ids=true, to_apply=%add | all-reduce | flops 4 | bytes 32
  28.9 0.0 copy-done
  28.9 0.1 copy.25
  29.1 0.1 fusion.23
  29.2 0.3 convolution_select_fusion
  29.5 1.2 convolution_bitcast_fusion
  30.7 67.0 %all-gather.13.cloned.1.call-done = f32[64,128,128]{2,1,0:T(8,128)} async-done(((f32[16,128,128]{2,1,0:T(8,128)}), f32[64,128,128]{2,1,0:T(8,128)}) %all-gather.13.cloned.1.call-update) | async-done | bytes 4194320 | tf_op jit(solution)/shard_map/all_gather | solution.py:16
  97.6 0.1 broadcast_in_dim.59
  97.7 0.0 copy-start.2
  97.8 3.3 multiply_reduce_fusion
  101.0 9.8 %psum.7 = f32[128]{0:T(128)S(1)} all-reduce(f32[128]{0:T(128)S(1)} %get-tuple-element.50), channel_id=1, replica_groups=mesh['section'=2,'seq'=4,'head'=4] {'head'}, use_global_device_ids=true, to_apply=%region_3.4 | all-reduce | flops 128 | bytes 1024 | tf_op jit(solution)/shard_map/psum | solution.py:89
  110.9 0.0 copy-done.2
  110.9 2.4 fusion.9
  113.3 0.0 all-gather.7.cloned.1.call-update
  113.3 0.0 copy-start.1
  113.3 0.0 reduce-scatter.2.cloned.1.call-start
  113.4 52.5 %all-gather.7.cloned.1.call-done = bf16[512,2048]{0,1:T(8,128)(2,1)} async-done(((bf16[128,2048]{0,1:T(8,128)(2,1)}), bf16[512,2048]{0,1:T(8,128)(2,1)}) %all-gather.7.cloned.1.call-update) | async-done | bytes 2097168 | tf_op jit(solution)/shard_map/all_gather | solution.py:94
  165.9 8.5 %fusion.2 = f32[512,1536]{1,0:T(8,128)} fusion(bf16[512,2048]{0,1:T(8,128)(2,1)} %all-gather.7.cloned.1.call-done, bf16[1,2048,1536]{2,1,0:T(8,128)(2,1)} %param.19), kind=kOutput, calls=%fused_computation.4 | convolution fusion | flops 3221225472 | bytes 11534336 | tf_op jit(solution)/shard_map/dot_general | solution.py:93
  174.4 0.0 copy-start.4
  174.4 0.0 reduce-scatter.2.cloned.1.call-update
  174.4 0.0 all-gather.9.cloned.1.call-start
  174.4 42.3 %reduce-scatter.2.cloned.1.call-done = f32[128,1536]{1,0:T(8,128)} async-done(((f32[512,1536]{1,0:T(8,128)}), f32[128,1536]{1,0:T(8,128)}) %reduce-scatter.2.cloned.1.call-update) | async-done | bytes 786448 | tf_op jit(solution)/shard_map/reduce_scatter | solution.py:101
  216.8 0.0 copy-done.1
  216.8 1.9 fusion.12
  218.7 0.0 all-gather.9.cloned.1.call-update
  218.7 0.2 all-gather.11.cloned.1.call-start
  219.0 31.0 %all-gather.9.cloned.1.call-done = bf16[512,1536]{1,0:T(8,128)(2,1)} async-done(((bf16[128,1536]{1,0:T(8,128)(2,1)}), bf16[512,1536]{1,0:T(8,128)(2,1)}) %all-gather.9.cloned.1.call-update) | async-done | bytes 1572880 | tf_op jit(solution)/shard_map/all_gather | solution.py:103
  250.0 0.0 all-gather.11.cloned.1.call-update
  250.0 0.1 collective-permute-start
  250.1 116.7 %all-gather.11.cloned.1.call-done = bf16[512,6144]{1,0:T(8,128)(2,1)} async-done(((bf16[512,1536]{1,0:T(8,128)(2,1)}), bf16[512,6144]{1,0:T(8,128)(2,1)}) %all-gather.11.cloned.1.call-update) | async-done | bytes 6291472 | tf_op jit(solution)/shard_map/all_gather | solution.py:105
  366.8 0.0 copy-done.4
  366.8 19.7 %bitcast_reduce_fusion = f32[8,2048]{1,0:T(8,128)S(1)} fusion(bf16[512,6144]{1,0:T(8,128)(2,1)} %all-gather.11.cloned.1.call-done, bf16[1,6144,2048]{2,1,0:T(8,128)(2,1)} %param.20, f32[2048]{0:T(1024)S(1)} %bitcast.80), kind=kOutput, calls=%fused_computation.6 | convolution fusion | flops 12888031232 | bytes 31531008 | tf_op jit(solution)/shard_map/dot_general | solution.py:104
  386.5 0.1 collective-permute-start.1
  386.7 0.0 collective-permute-done
  386.7 1.2 collective-permute-done.1
  387.8 0.7 copy.46
  388.6 0.6 copy.47
  (6 shorter events, 0.0 us)
Async XLA Ops:
  7.2 6.8 %copy-start.5 = (u32[32]{0:T(128)S(1)}, u32[32]{0:T(128)}, u32[]{:S(2)}) copy-start(u32[32]{0:T(128)} %constant.50) | copy-start | bytes 388
  7.2 7.4 %copy-start.3 = (s32[1,128]{1,0:T(1,128)S(1)}, s32[1,128]{1,0:T(1,128)}, u32[]{:S(2)}) copy-start(s32[1,128]{1,0:T(1,128)} %param.16) | copy-start | bytes 1540
  7.2 21.7 %copy-start = (bf16[1,128,2048]{2,1,0:T(8,128)(2,1)S(1)}, bf16[1,128,2048]{2,1,0:T(8,128)(2,1)}, u32[]{:S(2)}) copy-start(bf16[1,128,2048]{2,1,0:T(8,128)(2,1)} %param.12) | copy-start | bytes 1572868
  7.2 90.4 %all-gather.13.cloned.1.call-start = ((), (), s32[]{:S(2)}) async-start(), calls=%async_computation.5 | async-start | bytes 5242880 | tf_op jit(solution)/shard_map/all_gather | solution.py:16
  13.9 151.9 %all-gather.7.cloned.1.call-start = ((), (), s32[]{:S(2)}) async-start(), calls=%async_computation.1 | async-start | bytes 2621440 | tf_op jit(solution)/shard_map/all_gather | solution.py:94
  97.7 13.2 %copy-start.2 = (f32[1,2048]{1,0:T(1,128)S(1)}, f32[1,2048]{1,0:T(1,128)}, u32[]{:S(2)}) copy-start(f32[1,2048]{1,0:T(1,128)} %param.17) | copy-start | bytes 24580
  113.3 103.4 %copy-start.1 = (bf16[1,128,1536]{2,1,0:T(8,128)(2,1)S(1)}, bf16[1,128,1536]{2,1,0:T(8,128)(2,1)}, u32[]{:S(2)}) copy-start(bf16[1,128,1536]{2,1,0:T(8,128)(2,1)} %param.18) | copy-start | bytes 1179652
  113.3 103.4 %reduce-scatter.2.cloned.1.call-start = ((), (), s32[]{:S(2)}) async-start(), calls=%async_computation.2 | async-start | bytes 3932160 | tf_op jit(solution)/shard_map/reduce_scatter | solution.py:101
  174.4 192.4 %copy-start.4 = (f32[1,2048]{1,0:T(1,128)S(1)}, f32[1,2048]{1,0:T(1,128)}, u32[]{:S(2)}) copy-start(f32[1,2048]{1,0:T(1,128)} %param.21) | copy-start | bytes 24580
  174.4 75.6 %all-gather.9.cloned.1.call-start = ((), (), s32[]{:S(2)}) async-start(), calls=%async_computation.3 | async-start | bytes 1966080 | tf_op jit(solution)/shard_map/all_gather | solution.py:103
  218.7 148.1 %all-gather.11.cloned.1.call-start = ((), (), s32[]{:S(2)}) async-start(), calls=%async_computation.4 | async-start | bytes 7864320 | tf_op jit(solution)/shard_map/all_gather | solution.py:105
  250.0 136.6 %collective-permute-start = (bf16[1,128,1536]{2,1,0:T(8,128)(2,1)}, bf16[1,128,1536]{2,1,0:T(8,128)(2,1)S(1)}, u32[]{:S(2)}, u32[]{:S(2)}) collective-permute-start(bf16[1,128,1536]{2,1,0:T(8,128)(2,1)} %bitcast.76), channel_id=1, source_target_pairs={{0,16},{16,0},{1,17},{17,1},{2,18},{18,2},{3,19},{19,3},{4,20},{20... | collective-permute-start | bytes 1179656 | tf_op jit(solution)/shard_map/ppermute | solution.py:29
  386.5 1.3 collective-permute-start.1
Sparse Core Ops, SparseCore 0:
  14.1 83.5 all-gather.12
  113.4 52.3 all-gather.6
  174.5 42.1 reduce-scatter.1
  219.0 30.9 all-gather.8
  251.4 115.3 all-gather.10
where the time goes:
time: 396 us
  waiting for transfers between devices  311 us (79%)
  matrix products  34.4 us (9%)
  blocking collectives  23.4 us (6%)
  between operations  13.9 us (4%)
  local copies, waits for them, and re-layouts  6.9 us (2%)
  other arithmetic  5.77 us (1%)
    all_gather x1, waiting for transfers between devices, local(): lax.all_gather(features, 'seq', axis=1, tiled=True)  117 us
    all_gather x1, waiting for transfers between devices, entering(): gathered = jax.tree.map(lambda a: lax.all_gather(a, axis), part)  67 us
    all_gather x1, waiting for transfers between devices, local(): lax.all_gather(normed, 'seq', axis=0, tiled=True)  52.5 us
    reduce_scatter x1, waiting for transfers between devices, local(): lax.psum_scatter(partial_sums, 'head', scatter_dimension=0, tiled=True)  42.3 us
    all_gather x1, waiting for transfers between devices, local(): features = lax.all_gather(layer_out, 'head', axis=0, tiled=True)  31 us
    dot_general x1, matrix products, local(): jnp.dot(lax.all_gather(features, 'seq', axis=1, tiled=True), encoder, pre...  19.7 us
    unnamed x1, blocking collectives  13.5 us
    psum x1, blocking collectives, local(): total_square = lax.psum(jnp.sum(attended * attended, axis=1), 'head')  9.85 us
  transfers between devices with their start and end apart: 7, of which 6 were waited for; matrix products, arithmetic and copies ran while one was open for 6% of the time, Pallas kernels for 0%

commit v1 on v0

--- a/solution.py
+++ b/solution.py
@@ -1,6 +1,8 @@
 import jax
 import jax.numpy as jnp
 from jax import lax
+from jax.experimental import pallas as pl
+from jax.experimental.pallas import tpu as pltpu
 from jax.sharding import PartitionSpec as P
 
 HD = 128
@@ -112,9 +114,477 @@
     return (handoff, monitor)
 
 
+MESH = pl.DeviceIdType.MESH
+F32 = jnp.float32
+BF16 = jnp.bfloat16
+SEQ = 4
+GROUP = 4
+HALVES = 2
+HEAD_CHUNKS = 4
+
+
+def fused_kernel(
+    q_ref,
+    k_ref,
+    v_ref,
+    prior_ref,
+    doc_ref,
+    gain_ref,
+    res_ref,
+    ow_hbm,
+    enc_hbm,
+    bias_ref,
+    hand_ref,
+    mon_ref,
+    ow,
+    enc,
+    doc_own,
+    doc_prev,
+    state_in,
+    state_out,
+    summary,
+    attended,
+    sq_own,
+    sq_in,
+    rows,
+    part,
+    part_out,
+    part_in,
+    feats,
+    hand_in,
+    acc,
+    pool,
+    pool_in,
+    ow_sem,
+    enc_sem,
+    doc_sem,
+    st_s,
+    st_r,
+    sq_s,
+    sq_r,
+    row_s,
+    row_r,
+    part_s,
+    part_r,
+    zg_s,
+    zg_r,
+    x_s,
+    x_r,
+    y_s,
+    y_r,
+    d_s,
+    d_r,
+    hand_s,
+    hand_r,
+    pool_sem,
+):
+    s = lax.axis_index("section")
+    z = lax.axis_index("seq")
+    h = lax.axis_index("head")
+    tokens = q_ref.shape[1]
+    half = tokens // HALVES
+    heads = q_ref.shape[2] // HD
+    per_chunk = heads // HEAD_CHUNKS
+    width = res_ref.shape[2]
+    latents = bias_ref.shape[1]
+    x_peer = h + 1 - 2 * lax.rem(h, 2)
+    y_peer = lax.rem(h + 2, 4)
+    d_peer = 3 - h
+    mates = (x_peer, y_peer, d_peer)
+
+    def at(seq=None, head=None, section=None):
+        return (
+            s if section is None else section,
+            z if seq is None else seq,
+            h if head is None else head,
+        )
+
+    def remote(src, dst, send, recv, device):
+        return pltpu.make_async_remote_copy(
+            src_ref=src, dst_ref=dst, send_sem=send, recv_sem=recv,
+            device_id=device, device_id_type=MESH,
+        )
+
+    ow_copy = pltpu.make_async_copy(ow_hbm.at[0], ow, ow_sem)
+    enc_copy = pltpu.make_async_copy(enc_hbm.at[0], enc, enc_sem)
+    ow_copy.start()
+    enc_copy.start()
+
+    barrier = pltpu.get_barrier_semaphore()
+    for k in range(1, SEQ):
+        pl.semaphore_signal(barrier, inc=1, device_id=at(seq=lax.rem(z + k, SEQ)), device_id_type=MESH)
+    for mate in mates:
+        pl.semaphore_signal(barrier, inc=1, device_id=at(head=mate), device_id_type=MESH)
+    pl.semaphore_signal(barrier, inc=1, device_id=at(section=1 - s), device_id_type=MESH)
+    pl.semaphore_wait(barrier, SEQ - 1 + 3 + 1)
+
+    row_iota = lax.broadcasted_iota(jnp.int32, (tokens, tokens), 0)
+    col_iota = lax.broadcasted_iota(jnp.int32, (tokens, tokens), 1)
+    eye = row_iota == col_iota
+    doc_own[...] = jnp.broadcast_to(doc_ref[...].astype(F32), doc_own.shape)
+    later = jnp.minimum(z + 1, SEQ - 1)
+
+    def doc_copy():
+        return remote(doc_own, doc_prev, doc_sem.at[0], doc_sem.at[1], at(seq=later))
+
+    def state_copy(c):
+        return remote(state_out.at[c], state_in.at[c], st_s.at[c], st_r.at[c], at(seq=later))
+
+    @pl.when(z < SEQ - 1)
+    def _():
+        doc_copy().start()
+
+    doc_row = doc_own[0:1, :]
+    doc_col = jnp.sum(jnp.where(eye, doc_row, 0.0), axis=1, keepdims=True)
+    last_doc = jnp.max(doc_row, axis=1, keepdims=True)
+    keep_key = doc_col == last_doc
+    same_doc = (doc_col == doc_row) & (col_iota <= row_iota)
+
+    def columns(head):
+        return pl.ds(pl.multiple_of(head * HD, HD), HD)
+
+    def summarize(head, carry):
+        keys = k_ref[0, :, columns(head)]
+        keys = jnp.where(keep_key, keys.astype(F32), 0.0).astype(BF16)
+        summary[head] = lax.dot_general(
+            keys, v_ref[0, :, columns(head)], (((0,), (0,)), ((), ())), preferred_element_type=F32
+        )
+        return carry
+
+    def within(head, carry):
+        cols = columns(head)
+        values = v_ref[0, :, cols]
+        scores = lax.dot_general(
+            q_ref[0, :, cols], k_ref[0, :, cols], (((1,), (1,)), ((), ())), preferred_element_type=F32
+        )
+        scores = jnp.where(same_doc, scores, 0.0)
+        high = scores.astype(BF16)
+        low = (scores - high.astype(F32)).astype(BF16)
+        attended[:, cols] = jnp.dot(high, values, preferred_element_type=F32) + jnp.dot(
+            low, values, preferred_element_type=F32
+        )
+        return carry
+
+    lax.fori_loop(0, heads, summarize, 0)
+
+    @pl.when(z == 0)
+    def _():
+        doc_prev[...] = jnp.zeros_like(doc_prev)
+
+    @pl.when(z > 0)
+    def _():
+        doc_copy().wait_recv()
+
+    entering_doc = jnp.max(doc_prev[0:1, :], axis=1, keepdims=True)
+    carried = jnp.where(last_doc == entering_doc, 1.0, 0.0)
+    from_before = jnp.where(doc_col == entering_doc, 1.0, 0.0)
+
+    squares = jnp.zeros((tokens, HD), F32)
+    for c in range(HEAD_CHUNKS):
+        first = c * per_chunk
+
+        @pl.when(z == 0)
+        def _():
+            state_in[c] = prior_ref[0, first : first + per_chunk].astype(BF16)
+
+        if c > 0:
+            lax.fori_loop(first, first + per_chunk, within, 0)
+
+        @pl.when(z > 0)
+        def _():
+            state_copy(c).wait_recv()
+
+        @pl.when(z < SEQ - 1)
+        def _():
+            for i in range(per_chunk):
+                state_out[c, i] = (state_in[c, i].astype(F32) * carried + summary[first + i]).astype(BF16)
+            state_copy(c).start()
+
+        if c == 0:
+            lax.fori_loop(first, first + per_chunk, within, 0)
+
+        for i in range(per_chunk):
+            cols = slice((first + i) * HD, (first + i + 1) * HD)
+            inter = jnp.dot(q_ref[0, :, cols], state_in[c, i], preferred_element_type=F32)
+            total = attended[:, cols] + inter * from_before
+            attended[:, cols] = total
+            squares = squares + total * total
+
+    own_sum = jnp.sum(squares, axis=1, keepdims=True)
+    sq_own[...] = jnp.broadcast_to(
+        jnp.sum(jnp.where(eye, own_sum, 0.0), axis=0, keepdims=True), sq_own.shape
+    )
+
+    def sq_copy(i):
+        return remote(sq_own, sq_in.at[i], sq_s.at[i], sq_r.at[i], at(head=mates[i]))
+
+    for i in range(3):
+        sq_copy(i).start()
+    sum_row = sq_own[0:1, :]
+    for i in range(3):
+        sq_copy(i).wait_recv()
+        sum_row = sum_row + sq_in[i, 0:1, :]
+    sum_col = jnp.sum(jnp.where(eye, sum_row, 0.0), axis=1, keepdims=True)
+    inverse_rms = lax.rsqrt(sum_col / HDIM + epsilon)
+
+    def row_copy(c, k):
+        i = c * (SEQ - 1) + k - 1
+        return remote(
+            rows.at[c, z], rows.at[c, z], row_s.at[i], row_r.at[i], at(seq=lax.rem(z + k, SEQ))
+        )
+
+    for c in range(HALVES):
+        here = slice(c * half, (c + 1) * half)
+        rows[c, z] = (attended[here, :] * inverse_rms[here, :] * gain_ref[...]).astype(BF16)
+        for k in range(1, SEQ):
+            row_copy(c, k).start()
+
+    TILE = 256
+    depth = ow.shape[0]
+
+    def project(c):
+        for k in range(1, SEQ):
+            row_copy(c, k).wait_recv()
+
+        def one(n, carry):
+            cols = pl.ds(pl.multiple_of(n * TILE, TILE), TILE)
+            product = jnp.dot(
+                rows[c].reshape(SEQ * half, depth), ow[:, cols], preferred_element_type=F32
+            ).reshape(GROUP, half, TILE)
+            part[:, :, cols] = product
+            part_out[c, :, :, cols] = product.astype(BF16)
+            return carry
+
+        lax.fori_loop(0, width // TILE, one, 0)
+        for i in range(3):
+            part_copy(c, i).start()
+
+    def part_copy(c, i):
+        j = c * 3 + i
+        return remote(
+            part_out.at[c, mates[i]], part_in.at[c, i], part_s.at[j], part_r.at[j], at(head=mates[i])
+        )
+
+    def z_copy(c, k):
+        i = c * (SEQ - 1) + k - 1
+        block = feats.at[c, z, h]
+        return remote(block, block, zg_s.at[i], zg_r.at[i], at(seq=lax.rem(z + k, SEQ)))
+
+    def hand_copy(c):
+        return remote(feats.at[c, z, h], hand_in.at[c], hand_s.at[c], hand_r.at[c], at(section=1 - s))
+
+    def column(k):
+        return lax.rem(z + SEQ - k, SEQ)
+
+    def x_copy(c, k):
+        i = c * SEQ + k
+        block = feats.at[c, column(k), h]
+        return remote(block, block, x_s.at[i], x_r.at[i], at(head=x_peer))
+
+    def y_copy(c, k):
+        i = c * SEQ + k
+        block = feats.at[c, column(k), h]
+        return remote(block, block, y_s.at[i], y_r.at[i], at(head=y_peer))
+
+    def d_copy(c, k):
+        i = c * SEQ + k
+        source, target = (x_peer, y_peer) if k % 2 == 0 else (y_peer, x_peer)
+        block = feats.at[c, column(k), source]
+        return remote(block, block, d_s.at[i], d_r.at[i], at(head=target))
+
+    def finish(c):
+        here = slice(c * half, (c + 1) * half)
+        total = res_ref[0, here, :].astype(F32) + own_part[c]
+        for i in range(3):
+            part_copy(c, i).wait_recv()
+        for i in range(3):
+            total = total + part_in[c, i].astype(F32)
+        feats[c, z, h] = total.astype(BF16)
+        for k in (2, 1, 3):
+            z_copy(c, k).start()
+        x_copy(c, 0).start()
+        y_copy(c, 0).start()
+        hand_copy(c).start()
+
+    def relay(c, k):
+        if k > 0:
+            z_copy(c, k).wait_recv()
+            x_copy(c, k).start()
+            y_copy(c, k).start()
+
+    def forward(c, k):
+        (x_copy if k % 2 == 0 else y_copy)(c, k).wait_recv()
+        d_copy(c, k).start()
+
+    def encode(c, k):
+        (y_copy if k % 2 == 0 else x_copy)(c, k).wait_recv()
+        d_copy(c, k).wait_recv()
+        which = column(k)
+        depth_rows = pl.ds(pl.multiple_of(which * width, width), width)
+
+        def one(n, carry):
+            cols = pl.ds(pl.multiple_of(n * TILE, TILE), TILE)
+            product = jnp.dot(
+                feats[c, which].reshape(GROUP * half, width),
+                enc[depth_rows, cols],
+                preferred_element_type=F32,
+            )
+            if k == 0:
+                acc[:, cols] = product + bias_ref[:, cols]
+            elif k < SEQ - 1:
+                acc[:, cols] += product
+            else:
+                latent = jnp.maximum(acc[:, cols] + product, 0.0)
+                means = jnp.sum(latent.reshape(GROUP, half, TILE), axis=1) / POOL
+                for j in range(GROUP):
+                    pool[HALVES * j + c : HALVES * j + c + 1, cols] = means[j : j + 1, :]
+            return carry
+
+        lax.fori_loop(0, latents // TILE, one, 0)
+
+    own_part = {}
+    ow_copy.wait()
+    for c in range(HALVES):
+        project(c)
+        own_part[c] = part[h]
+        finish(c)
+    enc_copy.wait()
+    steps = [(c, k) for c in range(HALVES) for k in range(SEQ)]
+    lead, lag = 2, 3
+    for t in range(len(steps) + lag):
+        if t < len(steps):
+            relay(*steps[t])
+        if 0 <= t - lead < len(steps):
+            forward(*steps[t - lead])
+        if 0 <= t - lag < len(steps):
+            encode(*steps[t - lag])
+
+    pool_copy = remote(pool, pool_in, pool_sem.at[0], pool_sem.at[1], at(section=1 - s))
+    pool_copy.start()
+    for c in range(HALVES):
+        hand_copy(c).wait_recv()
+        hand_ref[0, c * half : (c + 1) * half, :] = hand_in[c]
+    pool_copy.wait_recv()
+    mon_ref[0] = pool_in[...].astype(BF16)
+
+    @pl.when(z < SEQ - 1)
+    def _():
+        doc_copy().wait_send()
+        for c in range(HEAD_CHUNKS):
+            state_copy(c).wait_send()
+
+    pool_copy.wait_send()
+    for i in range(3):
+        sq_copy(i).wait_send()
+    for c in range(HALVES):
+        hand_copy(c).wait_send()
+        for i in range(3):
+            part_copy(c, i).wait_send()
+        for k in range(1, SEQ):
+            row_copy(c, k).wait_send()
+            z_copy(c, k).wait_send()
+        for k in range(SEQ):
+            x_copy(c, k).wait_send()
+            y_copy(c, k).wait_send()
+            d_copy(c, k).wait_send()
+
+
+def fused(
+    query_vectors,
+    key_vectors,
+    value_vectors,
+    prior_state,
+    doc_ids,
+    norm_gain,
+    residual,
+    out_weight,
+    enc_weight,
+    enc_bias,
+):
+    tokens, features = query_vectors.shape[1:]
+    heads = features // HD
+    width = residual.shape[2]
+    depth, latents = enc_weight.shape[1:]
+    half = tokens // HALVES
+    per_chunk = heads // HEAD_CHUNKS
+    vmem = pl.BlockSpec(memory_space=pltpu.VMEM)
+    anywhere = pl.BlockSpec(memory_space=pl.ANY)
+    dma = lambda n: pltpu.SemaphoreType.DMA((n,))
+    buf = lambda shape, dtype: pltpu.VMEM(shape, dtype)
+    return pl.pallas_call(
+        fused_kernel,
+        out_shape=(
+            jax.ShapeDtypeStruct((1, tokens, width), BF16),
+            jax.ShapeDtypeStruct((1, SEQ * HALVES, latents), BF16),
+        ),
+        in_specs=[vmem] * 7 + [anywhere] * 2 + [vmem],
+        out_specs=(vmem, vmem),
+        scratch_shapes=[
+            buf((features, width), BF16),
+            buf((depth, latents), BF16),
+            buf((8, tokens), F32),
+            buf((8, tokens), F32),
+            buf((HEAD_CHUNKS, per_chunk, HD, HD), BF16),
+            buf((HEAD_CHUNKS, per_chunk, HD, HD), BF16),
+            buf((heads, HD, HD), F32),
+            buf((tokens, features), F32),
+            buf((8, tokens), F32),
+            buf((3, 8, tokens), F32),
+            buf((HALVES, SEQ, half, features), BF16),
+            buf((GROUP, half, width), F32),
+            buf((HALVES, GROUP, half, width), BF16),
+            buf((HALVES, 3, half, width), BF16),
+            buf((HALVES, SEQ, GROUP, half, width), BF16),
+            buf((HALVES, half, width), BF16),
+            buf((GROUP * half, latents), F32),
+            buf((SEQ * HALVES, latents), F32),
+            buf((SEQ * HALVES, latents), F32),
+            pltpu.SemaphoreType.DMA,
+            pltpu.SemaphoreType.DMA,
+            dma(2),
+            dma(HEAD_CHUNKS),
+            dma(HEAD_CHUNKS),
+            dma(3),
+            dma(3),
+            dma(HALVES * (SEQ - 1)),
+            dma(HALVES * (SEQ - 1)),
+            dma(HALVES * 3),
+            dma(HALVES * 3),
+            dma(HALVES * (SEQ - 1)),
+            dma(HALVES * (SEQ - 1)),
+            dma(HALVES * SEQ),
+            dma(HALVES * SEQ),
+            dma(HALVES * SEQ),
+            dma(HALVES * SEQ),
+            dma(HALVES * SEQ),
+            dma(HALVES * SEQ),
+            dma(HALVES),
+            dma(HALVES),
+            dma(2),
+        ],
+        compiler_params=pltpu.CompilerParams(
+            collective_id=0, has_side_effects=True, vmem_limit_bytes=60 * 2**20
+        ),
+        name="section",
+    )(
+        query_vectors,
+        key_vectors,
+        value_vectors,
+        prior_state,
+        doc_ids,
+        norm_gain,
+        residual,
+        out_weight,
+        enc_weight,
+        enc_bias,
+    )
+
+
 def solution(mesh):
+    sizes = (mesh.shape["section"], mesh.shape["seq"], mesh.shape["head"])
+    body = fused if sizes == (2, SEQ, GROUP) else local
     return jax.shard_map(
-        local,
+        body,
         mesh=mesh,
         in_specs=(
             P("section", "seq", "head"),

time: 396 us -> 162 us (0.41)
  the two profiles are of different devices: /device:TPU:0 before, /device:TPU:25 now
where the time goes in v1:
time: 162 us; the launch traced here: 161 us
  Pallas kernels  158 us (98%)
  local copies, waits for them, and re-layouts  3.14 us (2%)
    pallas_call x1, Pallas kernels, fused(): pl.pallas_call(fused_kernel, out_shape=(jax.ShapeDtypeStruct((1, tokens,...  158 us

profile of v1, /device:TPU:25, one launch (start us, length us, event | category | flops | bytes accessed | tf_op | source)
XLA Modules:
  0.0 161.4 jit_solution(9799497187956221426)
XLA Ops:
  0.6 157.6 %section.1 = (bf16[1,128,1536]{2,1,0:T(8,128)(2,1)}, bf16[1,8,2048]{2,1,0:T(8,128)(2,1)}) custom-call(bf16[1,128,2048]{2,1,0:T(8,128)(2,1)} %q_ref.1, bf16[1,128,2048]{2,1,0:T(8,128)(2,1)} %k_ref.1, bf16[1,128,2048]{2,1,0:T(8,128)(2,1)} %v_ref.1, f32[1,16,128,128]{3,2,1,0:T(8,128)} %prior_ref.1, s32[1,128]{1,0:T(1,128)} %doc_ref.1, f32[1,2048]{1,0:T(1,128)} %gain_ref.1, ...), custom_call_target="tpu_custom_call" | custom-call | tf_op jit(solution)/shard_map/section/pallas_call | solution.py:514
  158.3 1.8 %copy.14 = bf16[1,128,1536]{2,1,0:T(8,128)(2,1)} copy(bf16[1,128,1536]{2,1,0:T(8,128)(2,1)} %get-tuple-element.4) | data formatting | bytes 786432
  160.0 1.4 copy.15

commit v2 on v1

--- a/solution.py
+++ b/solution.py
@@ -119,8 +119,8 @@
 BF16 = jnp.bfloat16
 SEQ = 4
 GROUP = 4
-HALVES = 2
-HEAD_CHUNKS = 4
+CHUNKS = 4
+HEAD_GROUPS = 8
 
 
 def fused_kernel(
@@ -182,9 +182,9 @@
     z = lax.axis_index("seq")
     h = lax.axis_index("head")
     tokens = q_ref.shape[1]
-    half = tokens // HALVES
+    chunk_rows = tokens // CHUNKS
     heads = q_ref.shape[2] // HD
-    per_chunk = heads // HEAD_CHUNKS
+    per_chunk = heads // HEAD_GROUPS
     width = res_ref.shape[2]
     latents = bias_ref.shape[1]
     x_peer = h + 1 - 2 * lax.rem(h, 2)
@@ -241,17 +241,16 @@
     same_doc = (doc_col == doc_row) & (col_iota <= row_iota)
 
     def columns(head):
-        return pl.ds(pl.multiple_of(head * HD, HD), HD)
-
-    def summarize(head, carry):
+        return slice(head * HD, (head + 1) * HD)
+
+    def summarize(head):
         keys = k_ref[0, :, columns(head)]
         keys = jnp.where(keep_key, keys.astype(F32), 0.0).astype(BF16)
         summary[head] = lax.dot_general(
             keys, v_ref[0, :, columns(head)], (((0,), (0,)), ((), ())), preferred_element_type=F32
         )
-        return carry
-
-    def within(head, carry):
+
+    def within(head):
         cols = columns(head)
         values = v_ref[0, :, cols]
         scores = lax.dot_general(
@@ -263,9 +262,12 @@
         attended[:, cols] = jnp.dot(high, values, preferred_element_type=F32) + jnp.dot(
             low, values, preferred_element_type=F32
         )
-        return carry
-
-    lax.fori_loop(0, heads, summarize, 0)
+
+    def send_state(c):
+        for i in range(per_chunk):
+            head = c * per_chunk + i
+            state_out[c, i] = (state_in[c, i].astype(F32) * carried + summary[head]).astype(BF16)
+        state_copy(c).start()
 
     @pl.when(z == 0)
     def _():
@@ -279,32 +281,29 @@
     carried = jnp.where(last_doc == entering_doc, 1.0, 0.0)
     from_before = jnp.where(doc_col == entering_doc, 1.0, 0.0)
 
-    squares = jnp.zeros((tokens, HD), F32)
-    for c in range(HEAD_CHUNKS):
-        first = c * per_chunk
+    for c in range(HEAD_GROUPS):
+        for i in range(per_chunk):
+            summarize(c * per_chunk + i)
 
         @pl.when(z == 0)
         def _():
-            state_in[c] = prior_ref[0, first : first + per_chunk].astype(BF16)
-
-        if c > 0:
-            lax.fori_loop(first, first + per_chunk, within, 0)
-
+            state_in[c] = prior_ref[0, c * per_chunk : (c + 1) * per_chunk].astype(BF16)
+            send_state(c)
+
+    squares = jnp.zeros((tokens, HD), F32)
+    for c in range(HEAD_GROUPS):
         @pl.when(z > 0)
         def _():
             state_copy(c).wait_recv()
 
-        @pl.when(z < SEQ - 1)
+        @pl.when((z > 0) & (z < SEQ - 1))
         def _():
-            for i in range(per_chunk):
-                state_out[c, i] = (state_in[c, i].astype(F32) * carried + summary[first + i]).astype(BF16)
-            state_copy(c).start()
-
-        if c == 0:
-            lax.fori_loop(first, first + per_chunk, within, 0)
+            send_state(c)
 
         for i in range(per_chunk):
-            cols = slice((first + i) * HD, (first + i + 1) * HD)
+            head = c * per_chunk + i
+            cols = columns(head)
+            within(head)
             inter = jnp.dot(q_ref[0, :, cols], state_in[c, i], preferred_element_type=F32)
             total = attended[:, cols] + inter * from_before
             attended[:, cols] = total
@@ -333,11 +332,15 @@
             rows.at[c, z], rows.at[c, z], row_s.at[i], row_r.at[i], at(seq=lax.rem(z + k, SEQ))
         )
 
-    for c in range(HALVES):
-        here = slice(c * half, (c + 1) * half)
+    def push_rows(c):
+        for k in (2, 1, 3):
+            row_copy(c, k).start()
+
+    for c in range(CHUNKS):
+        here = slice(c * chunk_rows, (c + 1) * chunk_rows)
         rows[c, z] = (attended[here, :] * inverse_rms[here, :] * gain_ref[...]).astype(BF16)
-        for k in range(1, SEQ):
-            row_copy(c, k).start()
+        if c < 2:
+            push_rows(c)
 
     TILE = 256
     depth = ow.shape[0]
@@ -349,8 +352,8 @@
         def one(n, carry):
             cols = pl.ds(pl.multiple_of(n * TILE, TILE), TILE)
             product = jnp.dot(
-                rows[c].reshape(SEQ * half, depth), ow[:, cols], preferred_element_type=F32
-            ).reshape(GROUP, half, TILE)
+                rows[c].reshape(SEQ * chunk_rows, depth), ow[:, cols], preferred_element_type=F32
+            ).reshape(GROUP, chunk_rows, TILE)
             part[:, :, cols] = product
             part_out[c, :, :, cols] = product.astype(BF16)
             return carry
@@ -393,7 +396,7 @@
         return remote(block, block, d_s.at[i], d_r.at[i], at(head=target))
 
     def finish(c):
-        here = slice(c * half, (c + 1) * half)
+        here = slice(c * chunk_rows, (c + 1) * chunk_rows)
         total = res_ref[0, here, :].astype(F32) + own_part[c]
         for i in range(3):
             part_copy(c, i).wait_recv()
@@ -405,9 +408,11 @@
         x_copy(c, 0).start()
         y_copy(c, 0).start()
         hand_copy(c).start()
-
-    def relay(c, k):
-        if k > 0:
+        if c + 2 < CHUNKS:
+            push_rows(c + 2)
+
+    def relay(c):
+        for k in range(1, SEQ):
             z_copy(c, k).wait_recv()
             x_copy(c, k).start()
             y_copy(c, k).start()
@@ -425,7 +430,7 @@
         def one(n, carry):
             cols = pl.ds(pl.multiple_of(n * TILE, TILE), TILE)
             product = jnp.dot(
-                feats[c, which].reshape(GROUP * half, width),
+                feats[c, which].reshape(GROUP * chunk_rows, width),
                 enc[depth_rows, cols],
                 preferred_element_type=F32,
             )
@@ -435,48 +440,69 @@
                 acc[:, cols] += product
             else:
                 latent = jnp.maximum(acc[:, cols] + product, 0.0)
-                means = jnp.sum(latent.reshape(GROUP, half, TILE), axis=1) / POOL
+                sums = jnp.sum(latent.reshape(GROUP, chunk_rows, TILE), axis=1)
                 for j in range(GROUP):
-                    pool[HALVES * j + c : HALVES * j + c + 1, cols] = means[j : j + 1, :]
+                    r = (j * tokens + c * chunk_rows) // POOL
+                    row = sums[j : j + 1, :]
+                    if c * chunk_rows % POOL:
+                        row = row + pool[r : r + 1, cols]
+                    if (c + 1) * chunk_rows % POOL == 0:
+                        row = row / POOL
+                    pool[r : r + 1, cols] = row
             return carry
 
         lax.fori_loop(0, latents // TILE, one, 0)
 
     own_part = {}
-    ow_copy.wait()
-    for c in range(HALVES):
+
+    def produce(c):
         project(c)
         own_part[c] = part[h]
         finish(c)
+
+    def pass_on(c):
+        for k in range(SEQ):
+            forward(c, k)
+
+    ow_copy.wait()
+    produce(0)
+    produce(1)
+    relay(0)
+    pass_on(0)
+    produce(2)
+    relay(1)
+    pass_on(1)
+    produce(3)
+    relay(2)
     enc_copy.wait()
-    steps = [(c, k) for c in range(HALVES) for k in range(SEQ)]
-    lead, lag = 2, 3
-    for t in range(len(steps) + lag):
-        if t < len(steps):
-            relay(*steps[t])
-        if 0 <= t - lead < len(steps):
-            forward(*steps[t - lead])
-        if 0 <= t - lag < len(steps):
-            encode(*steps[t - lag])
+    for c in (0, 1):
+        if c == 1:
+            relay(3)
+        for k in range(SEQ):
+            encode(c, k)
+            forward(c + 2, k)
+    for c in (2, 3):
+        for k in range(SEQ):
+            encode(c, k)
 
     pool_copy = remote(pool, pool_in, pool_sem.at[0], pool_sem.at[1], at(section=1 - s))
     pool_copy.start()
-    for c in range(HALVES):
+    for c in range(CHUNKS):
         hand_copy(c).wait_recv()
-        hand_ref[0, c * half : (c + 1) * half, :] = hand_in[c]
+        hand_ref[0, c * chunk_rows : (c + 1) * chunk_rows, :] = hand_in[c]
     pool_copy.wait_recv()
     mon_ref[0] = pool_in[...].astype(BF16)
 
     @pl.when(z < SEQ - 1)
     def _():
         doc_copy().wait_send()
-        for c in range(HEAD_CHUNKS):
+        for c in range(HEAD_GROUPS):
             state_copy(c).wait_send()
 
     pool_copy.wait_send()
     for i in range(3):
         sq_copy(i).wait_send()
-    for c in range(HALVES):
+    for c in range(CHUNKS):
         hand_copy(c).wait_send()
         for i in range(3):
             part_copy(c, i).wait_send()
@@ -505,8 +531,8 @@
     heads = features // HD
     width = residual.shape[2]
     depth, latents = enc_weight.shape[1:]
-    half = tokens // HALVES
-    per_chunk = heads // HEAD_CHUNKS
+    chunk_rows = tokens // CHUNKS
+    per_chunk = heads // HEAD_GROUPS
     vmem = pl.BlockSpec(memory_space=pltpu.VMEM)
     anywhere = pl.BlockSpec(memory_space=pl.ANY)
     dma = lambda n: pltpu.SemaphoreType.DMA((n,))
@@ -515,7 +541,7 @@
         fused_kernel,
         out_shape=(
             jax.ShapeDtypeStruct((1, tokens, width), BF16),
-            jax.ShapeDtypeStruct((1, SEQ * HALVES, latents), BF16),
+            jax.ShapeDtypeStruct((1, SEQ * tokens // POOL, latents), BF16),
         ),
         in_specs=[vmem] * 7 + [anywhere] * 2 + [vmem],
         out_specs=(vmem, vmem),
@@ -524,42 +550,42 @@
             buf((depth, latents), BF16),
             buf((8, tokens), F32),
             buf((8, tokens), F32),
-            buf((HEAD_CHUNKS, per_chunk, HD, HD), BF16),
-            buf((HEAD_CHUNKS, per_chunk, HD, HD), BF16),
+            buf((HEAD_GROUPS, per_chunk, HD, HD), BF16),
+            buf((HEAD_GROUPS, per_chunk, HD, HD), BF16),
             buf((heads, HD, HD), F32),
             buf((tokens, features), F32),
             buf((8, tokens), F32),
             buf((3, 8, tokens), F32),
-            buf((HALVES, SEQ, half, features), BF16),
-            buf((GROUP, half, width), F32),
-            buf((HALVES, GROUP, half, width), BF16),
-            buf((HALVES, 3, half, width), BF16),
-            buf((HALVES, SEQ, GROUP, half, width), BF16),
-            buf((HALVES, half, width), BF16),
-            buf((GROUP * half, latents), F32),
-            buf((SEQ * HALVES, latents), F32),
-            buf((SEQ * HALVES, latents), F32),
+            buf((CHUNKS, SEQ, chunk_rows, features), BF16),
+            buf((GROUP, chunk_rows, width), F32),
+            buf((CHUNKS, GROUP, chunk_rows, width), BF16),
+            buf((CHUNKS, 3, chunk_rows, width), BF16),
+            buf((CHUNKS, SEQ, GROUP, chunk_rows, width), BF16),
+            buf((CHUNKS, chunk_rows, width), BF16),
+            buf((GROUP * chunk_rows, latents), F32),
+            buf((SEQ * tokens // POOL, latents), F32),
+            buf((SEQ * tokens // POOL, latents), F32),
             pltpu.SemaphoreType.DMA,
             pltpu.SemaphoreType.DMA,
             dma(2),
-            dma(HEAD_CHUNKS),
-            dma(HEAD_CHUNKS),
+            dma(HEAD_GROUPS),
+            dma(HEAD_GROUPS),
             dma(3),
             dma(3),
-            dma(HALVES * (SEQ - 1)),
-            dma(HALVES * (SEQ - 1)),
-            dma(HALVES * 3),
-            dma(HALVES * 3),
-            dma(HALVES * (SEQ - 1)),
-            dma(HALVES * (SEQ - 1)),
-            dma(HALVES * SEQ),
-            dma(HALVES * SEQ),
-            dma(HALVES * SEQ),
-            dma(HALVES * SEQ),
-            dma(HALVES * SEQ),
-            dma(HALVES * SEQ),
-            dma(HALVES),
-            dma(HALVES),
+            dma(CHUNKS * (SEQ - 1)),
+            dma(CHUNKS * (SEQ - 1)),
+            dma(CHUNKS * 3),
+            dma(CHUNKS * 3),
+            dma(CHUNKS * (SEQ - 1)),
+            dma(CHUNKS * (SEQ - 1)),
+            dma(CHUNKS * SEQ),
+            dma(CHUNKS * SEQ),
+            dma(CHUNKS * SEQ),
+            dma(CHUNKS * SEQ),
+            dma(CHUNKS * SEQ),
+            dma(CHUNKS * SEQ),
+            dma(CHUNKS),
+            dma(CHUNKS),
             dma(2),
         ],
         compiler_params=pltpu.CompilerParams(

time: 162 us -> 164 us (1.012)
  the two profiles are of different devices: /device:TPU:25 before, /device:TPU:0 now
where the time goes in v2:
time: 164 us; the launch traced here: 162 us
  Pallas kernels  158 us (96%)
  local copies, waits for them, and re-layouts  3.14 us (2%)
    pallas_call x1, Pallas kernels, fused(): pl.pallas_call(fused_kernel, out_shape=(jax.ShapeDtypeStruct((1, tokens,...  158 us

profile of v2, /device:TPU:0, one launch (start us, length us, event | category | flops | bytes accessed | tf_op | source)
XLA Modules:
  0.0 162.1 jit_solution(2994258097989133710)
XLA Ops:
  0.6 158.3 %section.1 = (bf16[1,128,1536]{2,1,0:T(8,128)(2,1)}, bf16[1,8,2048]{2,1,0:T(8,128)(2,1)}) custom-call(bf16[1,128,2048]{2,1,0:T(8,128)(2,1)} %q_ref.1, bf16[1,128,2048]{2,1,0:T(8,128)(2,1)} %k_ref.1, bf16[1,128,2048]{2,1,0:T(8,128)(2,1)} %v_ref.1, f32[1,16,128,128]{3,2,1,0:T(8,128)} %prior_ref.1, s32[1,128]{1,0:T(1,128)} %doc_ref.1, f32[1,2048]{1,0:T(1,128)} %gain_ref.1, ...), custom_call_target="tpu_custom_call" | custom-call | tf_op jit(solution)/shard_map/section/pallas_call | solution.py:540
  158.9 1.8 %copy.14 = bf16[1,128,1536]{2,1,0:T(8,128)(2,1)} copy(bf16[1,128,1536]{2,1,0:T(8,128)(2,1)} %get-tuple-element.4) | data formatting | bytes 786432
  160.7 1.4 copy.15

commit v3 on v2

--- a/solution.py
+++ b/solution.py
@@ -332,9 +332,58 @@
             rows.at[c, z], rows.at[c, z], row_s.at[i], row_r.at[i], at(seq=lax.rem(z + k, SEQ))
         )
 
+    inner = (z > 0) & (z < SEQ - 1)
+    direct = {1: z != SEQ - 1, 2: z >= 0, 3: z != 0}
+    relay_target = lax.rem(jnp.maximum(z - 1, 0), 2) * (SEQ - 1)
+    relay_sem = lax.rem(2 * z + SEQ - 2, SEQ)
+    relay_block = lax.rem(z + 2, SEQ)
+
+    def start_along(copy, c):
+        copy(c, 2).start()
+        for k in (1, 3):
+
+            @pl.when(direct[k])
+            def _():
+                copy(c, k).start()
+
+    def wait_along(copy, relayed, c):
+        copy(c, 2).wait_recv()
+
+        @pl.when(inner)
+        def _():
+            relayed(c).start()
+
+        for k in (1, 3):
+            copy(c, k).wait_recv()
+
+    def sent_along(copy, relayed, c):
+        copy(c, 2).wait_send()
+        for k in (1, 3):
+
+            @pl.when(direct[k])
+            def _():
+                copy(c, k).wait_send()
+
+        @pl.when(inner)
+        def _():
+            relayed(c).wait_send()
+
+    def row_relay(c):
+        block = rows.at[c, relay_block]
+        return remote(
+            block, block, row_s.at[CHUNKS * (SEQ - 1) + c],
+            row_r.at[c * (SEQ - 1) + relay_sem], at(seq=relay_target),
+        )
+
+    def z_relay(c):
+        block = feats.at[c, relay_block, h]
+        return remote(
+            block, block, zg_s.at[CHUNKS * (SEQ - 1) + c],
+            zg_r.at[c * (SEQ - 1) + relay_sem], at(seq=relay_target),
+        )
+
     def push_rows(c):
-        for k in (2, 1, 3):
-            row_copy(c, k).start()
+        start_along(row_copy, c)
 
     for c in range(CHUNKS):
         here = slice(c * chunk_rows, (c + 1) * chunk_rows)
@@ -346,8 +395,7 @@
     depth = ow.shape[0]
 
     def project(c):
-        for k in range(1, SEQ):
-            row_copy(c, k).wait_recv()
+        wait_along(row_copy, row_relay, c)
 
         def one(n, carry):
             cols = pl.ds(pl.multiple_of(n * TILE, TILE), TILE)
@@ -403,8 +451,7 @@
         for i in range(3):
             total = total + part_in[c, i].astype(F32)
         feats[c, z, h] = total.astype(BF16)
-        for k in (2, 1, 3):
-            z_copy(c, k).start()
+        start_along(z_copy, c)
         x_copy(c, 0).start()
         y_copy(c, 0).start()
         hand_copy(c).start()
@@ -412,8 +459,8 @@
             push_rows(c + 2)
 
     def relay(c):
+        wait_along(z_copy, z_relay, c)
         for k in range(1, SEQ):
-            z_copy(c, k).wait_recv()
             x_copy(c, k).start()
             y_copy(c, k).start()
 
@@ -472,15 +519,21 @@
     produce(2)
     relay(1)
     pass_on(1)
+    enc_copy.wait()
+    encode(0, 0)
+    encode(0, 1)
     produce(3)
     relay(2)
-    enc_copy.wait()
-    for c in (0, 1):
-        if c == 1:
-            relay(3)
-        for k in range(SEQ):
-            encode(c, k)
-            forward(c + 2, k)
+    forward(2, 0)
+    forward(2, 1)
+    encode(0, 2)
+    forward(2, 2)
+    encode(0, 3)
+    forward(2, 3)
+    relay(3)
+    for k in range(SEQ):
+        forward(3, k)
+        encode(1, k)
     for c in (2, 3):
         for k in range(SEQ):
             encode(c, k)
@@ -506,9 +559,8 @@
         hand_copy(c).wait_send()
         for i in range(3):
             part_copy(c, i).wait_send()
-        for k in range(1, SEQ):
-            row_copy(c, k).wait_send()
-            z_copy(c, k).wait_send()
+        sent_along(row_copy, row_relay, c)
+        sent_along(z_copy, z_relay, c)
         for k in range(SEQ):
             x_copy(c, k).wait_send()
             y_copy(c, k).wait_send()
@@ -572,11 +624,11 @@
             dma(HEAD_GROUPS),
             dma(3),
             dma(3),
-            dma(CHUNKS * (SEQ - 1)),
+            dma(CHUNKS * SEQ),
             dma(CHUNKS * (SEQ - 1)),
             dma(CHUNKS * 3),
             dma(CHUNKS * 3),
-            dma(CHUNKS * (SEQ - 1)),
+            dma(CHUNKS * SEQ),
             dma(CHUNKS * (SEQ - 1)),
             dma(CHUNKS * SEQ),
             dma(CHUNKS * SEQ),

time: 164 us -> 160 us (0.976); the launches traced: 162 us -> 160 us
  Pallas kernels: 158 us -> 156 us
    pallas_call x1, Pallas kernels: 158 us -> 156 us  [fused(): pl.pallas_call(fused_kernel, out_shape=(jax.ShapeDtypeStruct((1, tokens,...]
where the time goes in v3:
time: 160 us
  Pallas kernels  156 us (98%)
  local copies, waits for them, and re-layouts  3.14 us (2%)
    pallas_call x1, Pallas kernels, fused(): pl.pallas_call(fused_kernel, out_shape=(jax.ShapeDtypeStruct((1, tokens,...  156 us

profile of v3, /device:TPU:0, one launch (start us, length us, event | category | flops | bytes accessed | tf_op | source)
XLA Modules:
  0.0 160.0 jit_solution(3141516875537576033)
XLA Ops:
  0.6 156.2 %section.1 = (bf16[1,128,1536]{2,1,0:T(8,128)(2,1)}, bf16[1,8,2048]{2,1,0:T(8,128)(2,1)}) custom-call(bf16[1,128,2048]{2,1,0:T(8,128)(2,1)} %q_ref.1, bf16[1,128,2048]{2,1,0:T(8,128)(2,1)} %k_ref.1, bf16[1,128,2048]{2,1,0:T(8,128)(2,1)} %v_ref.1, f32[1,16,128,128]{3,2,1,0:T(8,128)} %prior_ref.1, s32[1,128]{1,0:T(1,128)} %doc_ref.1, f32[1,2048]{1,0:T(1,128)} %gain_ref.1, ...), custom_call_target="tpu_custom_call" | custom-call | tf_op jit(solution)/shard_map/section/pallas_call | solution.py:592
  156.8 1.8 %copy.14 = bf16[1,128,1536]{2,1,0:T(8,128)(2,1)} copy(bf16[1,128,1536]{2,1,0:T(8,128)(2,1)} %get-tuple-element.4) | data formatting | bytes 786432
  158.6 1.4 copy.15

commit v4 on v3

--- a/solution.py
+++ b/solution.py
@@ -205,10 +205,16 @@
             device_id=device, device_id_type=MESH,
         )
 
+    def column(k):
+        return lax.rem(z + SEQ - k, SEQ)
+
     ow_copy = pltpu.make_async_copy(ow_hbm.at[0], ow, ow_sem)
-    enc_copy = pltpu.make_async_copy(enc_hbm.at[0], enc, enc_sem)
     ow_copy.start()
-    enc_copy.start()
+
+    def enc_copy(k):
+        which = column(k)
+        place = pl.ds(pl.multiple_of(which * width, width), width)
+        return pltpu.make_async_copy(enc_hbm.at[0, place], enc.at[place], enc_sem.at[k])
 
     barrier = pltpu.get_barrier_semaphore()
     for k in range(1, SEQ):
@@ -398,15 +404,16 @@
         wait_along(row_copy, row_relay, c)
 
         def one(n, carry):
-            cols = pl.ds(pl.multiple_of(n * TILE, TILE), TILE)
-            product = jnp.dot(
-                rows[c].reshape(SEQ * chunk_rows, depth), ow[:, cols], preferred_element_type=F32
-            ).reshape(GROUP, chunk_rows, TILE)
-            part[:, :, cols] = product
-            part_out[c, :, :, cols] = product.astype(BF16)
+            for u in range(3):
+                cols = pl.ds(pl.multiple_of((n * 3 + u) * TILE, TILE), TILE)
+                product = jnp.dot(
+                    rows[c].reshape(SEQ * chunk_rows, depth), ow[:, cols], preferred_element_type=F32
+                ).reshape(GROUP, chunk_rows, TILE)
+                part[:, :, cols] = product
+                part_out[c, :, :, cols] = product.astype(BF16)
             return carry
 
-        lax.fori_loop(0, width // TILE, one, 0)
+        lax.fori_loop(0, width // (3 * TILE), one, 0)
         for i in range(3):
             part_copy(c, i).start()
 
@@ -423,9 +430,6 @@
 
     def hand_copy(c):
         return remote(feats.at[c, z, h], hand_in.at[c], hand_s.at[c], hand_r.at[c], at(section=1 - s))
-
-    def column(k):
-        return lax.rem(z + SEQ - k, SEQ)
 
     def x_copy(c, k):
         i = c * SEQ + k
@@ -468,42 +472,43 @@
         (x_copy if k % 2 == 0 else y_copy)(c, k).wait_recv()
         d_copy(c, k).start()
 
-    def encode(c, k):
-        (y_copy if k % 2 == 0 else x_copy)(c, k).wait_recv()
-        d_copy(c, k).wait_recv()
+    def encode(p, k):
+        for c in (2 * p, 2 * p + 1):
+            (y_copy if k % 2 == 0 else x_copy)(c, k).wait_recv()
+            d_copy(c, k).wait_recv()
         which = column(k)
         depth_rows = pl.ds(pl.multiple_of(which * width, width), width)
+        if p == 0:
+            enc_copy(k).wait()
 
         def one(n, carry):
-            cols = pl.ds(pl.multiple_of(n * TILE, TILE), TILE)
-            product = jnp.dot(
-                feats[c, which].reshape(GROUP * chunk_rows, width),
-                enc[depth_rows, cols],
-                preferred_element_type=F32,
-            )
-            if k == 0:
-                acc[:, cols] = product + bias_ref[:, cols]
-            elif k < SEQ - 1:
-                acc[:, cols] += product
-            else:
-                latent = jnp.maximum(acc[:, cols] + product, 0.0)
-                sums = jnp.sum(latent.reshape(GROUP, chunk_rows, TILE), axis=1)
-                for j in range(GROUP):
-                    r = (j * tokens + c * chunk_rows) // POOL
-                    row = sums[j : j + 1, :]
-                    if c * chunk_rows % POOL:
-                        row = row + pool[r : r + 1, cols]
-                    if (c + 1) * chunk_rows % POOL == 0:
-                        row = row / POOL
-                    pool[r : r + 1, cols] = row
+            for u in range(4):
+                cols = pl.ds(pl.multiple_of((n * 4 + u) * TILE, TILE), TILE)
+                product = jnp.dot(
+                    feats[2 * p : 2 * p + 2, which].reshape(2 * GROUP * chunk_rows, width),
+                    enc[depth_rows, cols],
+                    preferred_element_type=F32,
+                )
+                if k == 0:
+                    acc[:, cols] = product + bias_ref[:, cols]
+                elif k < SEQ - 1:
+                    acc[:, cols] += product
+                else:
+                    latent = jnp.maximum(acc[:, cols] + product, 0.0)
+                    latent = latent.reshape(2, GROUP, chunk_rows, TILE)
+                    means = jnp.sum(latent[0] + latent[1], axis=1) / POOL
+                    for j in range(GROUP):
+                        r = j * (tokens // POOL) + p
+                        pool[r : r + 1, cols] = means[j : j + 1, :]
             return carry
 
-        lax.fori_loop(0, latents // TILE, one, 0)
+        lax.fori_loop(0, latents // (4 * TILE), one, 0)
 
     own_part = {}
 
     def produce(c):
         project(c)
+        enc_copy(c).start()
         own_part[c] = part[h]
         finish(c)
 
@@ -519,24 +524,20 @@
     produce(2)
     relay(1)
     pass_on(1)
-    enc_copy.wait()
+    produce(3)
+    relay(2)
+    pass_on(2)
     encode(0, 0)
     encode(0, 1)
-    produce(3)
-    relay(2)
-    forward(2, 0)
-    forward(2, 1)
+    relay(3)
     encode(0, 2)
-    forward(2, 2)
+    forward(3, 0)
+    forward(3, 1)
     encode(0, 3)
-    forward(2, 3)
-    relay(3)
+    forward(3, 2)
+    forward(3, 3)
     for k in range(SEQ):
-        forward(3, k)
         encode(1, k)
-    for c in (2, 3):
-        for k in range(SEQ):
-            encode(c, k)
 
     pool_copy = remote(pool, pool_in, pool_sem.at[0], pool_sem.at[1], at(section=1 - s))
     pool_copy.start()
@@ -614,11 +615,11 @@
             buf((CHUNKS, 3, chunk_rows, width), BF16),
             buf((CHUNKS, SEQ, GROUP, chunk_rows, width), BF16),
             buf((CHUNKS, chunk_rows, width), BF16),
-            buf((GROUP * chunk_rows, latents), F32),
+            buf((2 * GROUP * chunk_rows, latents), F32),
             buf((SEQ * tokens // POOL, latents), F32),
             buf((SEQ * tokens // POOL, latents), F32),
             pltpu.SemaphoreType.DMA,
-            pltpu.SemaphoreType.DMA,
+            dma(SEQ),
             dma(2),
             dma(HEAD_GROUPS),
             dma(HEAD_GROUPS),

time: 160 us -> 145 us (0.906)
  Pallas kernels: 156 us -> 141 us
    pallas_call x1, Pallas kernels: 156 us -> 141 us  [fused(): pl.pallas_call(fused_kernel, out_shape=(jax.ShapeDtypeStruct((1, tokens,...]
where the time goes in v4:
time: 145 us
  Pallas kernels  141 us (97%)
  local copies, waits for them, and re-layouts  3.14 us (2%)
    pallas_call x1, Pallas kernels, fused(): pl.pallas_call(fused_kernel, out_shape=(jax.ShapeDtypeStruct((1, tokens,...  141 us
    unnamed x2, local copies, waits for them, and re-layouts  3.14 us

profile of v4, /device:TPU:0, one launch (start us, length us, event | category | flops | bytes accessed | tf_op | source)
XLA Modules:
  0.0 145.2 jit_solution(764817164699276190)
XLA Ops:
  0.6 141.5 %section.1 = (bf16[1,128,1536]{2,1,0:T(8,128)(2,1)}, bf16[1,8,2048]{2,1,0:T(8,128)(2,1)}) custom-call(bf16[1,128,2048]{2,1,0:T(8,128)(2,1)} %q_ref.1, bf16[1,128,2048]{2,1,0:T(8,128)(2,1)} %k_ref.1, bf16[1,128,2048]{2,1,0:T(8,128)(2,1)} %v_ref.1, f32[1,16,128,128]{3,2,1,0:T(8,128)} %prior_ref.1, s32[1,128]{1,0:T(1,128)} %doc_ref.1, f32[1,2048]{1,0:T(1,128)} %gain_ref.1, ...), custom_call_target="tpu_custom_call" | custom-call | tf_op jit(solution)/shard_map/section/pallas_call | solution.py:593
  142.1 1.8 %copy.14 = bf16[1,128,1536]{2,1,0:T(8,128)(2,1)} copy(bf16[1,128,1536]{2,1,0:T(8,128)(2,1)} %get-tuple-element.4) | data formatting | bytes 786432
  143.9 1.4 copy.15
